TPU v7x, 256 devices: a whole 4x4x8 slice. The times are simulated.
256 devices in a mesh: tg: 4 (over y), pl: 64 (over x, z, core).
Axes of the slice: x: 4, y: 4, z: 8, core: 2. Of those that a mesh axis runs over, the one named last changes fastest.
Arguments:
- coeffs: float32 [2, 4, 8192, 128], P(None, None, ('tg', 'pl')), may hold values from -6 to 6
- potential: float32 [256, 256, 256], P('pl'), may hold values from -2 to 1
- stick_x: int32 [8192], P(('tg', 'pl')), may hold values from 0 to 255, as said below
- stick_y: int32 [8192], P(('tg', 'pl')), may hold values from 0 to 255, as said below
- stick_count: int32 [8192], P(('tg', 'pl')), may hold values from 0 to 128, as said below
- stick_offset: int32 [8192], P(('tg', 'pl')), may hold values from 0 to 255, as said below
Outputs:
- hpsi: float32 [2, 4, 8192, 128], P(None, None, ('tg', 'pl'))
Inputs may be any that keep to these rules, and one draw needn't show every extreme that they name: The columns stick_x * 256 + stick_y of all 8192 sticks are distinct. `stick_y`: a stick with count 1 or more has signed column frequencies fx, fy with fx^2 + fy^2 <= 64^2; a stick with count 0 lies outside that disk. `stick_count`: a live stick's count is min(128, 2 * floor(sqrt(64^2 - fx^2 - fy^2)) + 1); on each device's 32 slots the live sticks come first; one device has all 32 slots live and its first stick is the column (0, 0) with 128 G-vectors; every other device has between 16 and 20 live sticks. stick_offset = (-(stick_count // 2)) mod 256, so each stick's G-vectors are centred on z = 0.
All inputs are finite; a program needn't handle non-finite values.
Results may differ from a plain program's by a relative error of at most 0.0002.
Values sent between devices are 32-bit elements; how exact they have to be, the bound alone decides.
A program may use at most 128 MiB of HBM per device.

v0:
```python
import functools
import math

import jax
import jax.numpy as jnp
import numpy as np
from jax import lax
from jax.experimental import pallas as pl
from jax.experimental.pallas import tpu as pltpu
from jax.sharding import PartitionSpec as P

BF = jnp.bfloat16
F32 = jnp.float32
MESH = pl.DeviceIdType.MESH

NG = 256
DEPTH = 128
SLOT = 32
GROUPS = 4
PLANES = 64
LAYERS = 4
ROWS = 2 * LAYERS
KEPT = 128
STEP = 8


def halves(table):
    import ml_dtypes

    high = table.astype(ml_dtypes.bfloat16)
    low = (table - high.astype(np.float64)).astype(ml_dtypes.bfloat16)
    return np.stack([high, low])


def angles(rows, cols):
    return (np.multiply.outer(rows, cols) % NG) * (2.0 * math.pi / NG)


@functools.lru_cache(None)
def tables():
    angle = angles(np.arange(NG), np.arange(DEPTH)).reshape(PLANES, LAYERS, DEPTH)
    cos, sin = np.cos(angle), np.sin(angle)
    real = np.concatenate([cos, -sin], -1)
    imag = np.concatenate([sin, cos], -1)
    straight = np.concatenate([real, imag], 1).reshape(-1, 2 * DEPTH)
    turned = np.concatenate([-imag, real], 1).reshape(-1, 2 * DEPTH)
    lines = np.concatenate([straight, turned])
    angle = angles(np.arange(NG), np.arange(NG)).reshape(PLANES, LAYERS, NG)
    double = lambda t: np.concatenate([t, t], 1).reshape(-1, NG)
    phase = np.concatenate([double(np.cos(angle)), double(np.sin(angle))])
    freq = np.arange(KEPT) - KEPT // 2
    split = np.concatenate([freq[0::2], freq[1::2]])
    angle = angles(np.arange(NG), split)
    cos, sin = np.cos(angle), np.sin(angle)
    along_x = np.block([[cos, -sin], [sin, cos]])
    angle = angles(freq, np.arange(NG))
    cos, sin = np.cos(angle), np.sin(angle)
    along_y = np.block([[cos, sin], [-sin, cos]])
    scale = 1.0 / float(NG) ** 3
    return tuple(
        halves(t)
        for t in (lines, lines.T * scale, phase, along_x, along_x.T, along_y, along_y.T)
    )


def split(values):
    high = values.astype(BF)
    return high, (values - high.astype(F32)).astype(BF)


def dot(a, b):
    return jnp.dot(a, b, preferred_element_type=F32)


def dot3(a, b):
    return dot(a[0], b[0]) + (dot(a[0], b[1]) + dot(a[1], b[0]))


def quarter(index):
    index = index & 3
    one, zero = jnp.float32(1.0), jnp.float32(0.0)
    cos = jnp.where(index == 0, one, jnp.where(index == 2, -one, zero))
    sin = jnp.where(index == 1, one, jnp.where(index == 3, -one, zero))
    return cos, sin


def kernel(
    coeffs,
    meta,
    potential,
    lines_hbm,
    lines_t_hbm,
    phase_hbm,
    ax_hbm,
    axt_hbm,
    ay_hbm,
    ayt_hbm,
    result,
    group,
    metas,
    pot,
    lines,
    lines_t,
    phase,
    ax,
    axt,
    ay,
    ayt,
    send,
    recv,
    phases,
    onehot,
    spread,
    plane,
    psi,
    fields,
    sback,
    ret,
    back,
    local_sem,
    tg_send,
    tg_recv,
    out_send,
    out_recv,
    meta_send,
    meta_recv,
    pl_send,
    pl_recv,
    rt_send,
    rt_recv,
):
    tg = lax.axis_index("tg")
    me = lax.axis_index("pl")
    fetches = [
        pltpu.make_async_copy(src, dst, local_sem.at[i])
        for i, (src, dst) in enumerate(
            [
                (coeffs.at[:, tg], group.at[:, tg]),
                (phase_hbm, phase),
                (lines_hbm, lines),
                (ax_hbm, ax),
                (ay_hbm, ay),
                (potential, pot),
                (ayt_hbm, ayt),
                (axt_hbm, axt),
                (lines_t_hbm, lines_t),
            ]
        )
    ]
    for fetch in fetches:
        fetch.start()

    barrier = pltpu.get_barrier_semaphore()
    for step in range(1, GROUPS):
        pl.semaphore_signal(
            barrier, inc=1, device_id=(lax.rem(tg + step, GROUPS), me), device_id_type=MESH
        )

    def greet(step, carry):
        pl.semaphore_signal(
            barrier, inc=1, device_id=(tg, lax.rem(me + step, PLANES)), device_id_type=MESH
        )
        return carry

    lax.fori_loop(1, PLANES, greet, 0)
    pl.semaphore_wait(barrier, GROUPS - 1 + PLANES - 1)

    copies = []
    for step in range(1, GROUPS):
        other = lax.rem(tg + step, GROUPS)
        for src, dst, sems in (
            (meta, metas.at[step], (meta_send, meta_recv)),
            (coeffs.at[:, other], group.at[:, tg], (tg_send, tg_recv)),
        ):
            copy = pltpu.make_async_remote_copy(
                src_ref=src,
                dst_ref=dst,
                send_sem=sems[0].at[step],
                recv_sem=sems[1].at[step],
                device_id=(other, me),
                device_id_type=MESH,
            )
            copy.start()
            copies.append(copy)
    for copy in copies[0::2]:
        copy.wait()
    info = meta[...] + metas[1] + metas[2] + metas[3]
    ids, count, offset = info[0:1], info[1:2], info[2:3]
    fetches[1].wait()
    steps = lax.broadcasted_iota(jnp.int32, (NG, 128), 0).astype(F32)
    chosen = jnp.where(steps == offset, 1.0, 0.0).astype(BF)
    phases[...] = dot(phase[0], chosen) + dot(phase[1], chosen)
    fetches[0].wait()
    fetches[2].wait()
    for copy in copies[1::2]:
        copy.wait()

    live = steps[:DEPTH] < count
    parts = []
    for part in range(2):
        rows = group[part].reshape(GROUPS * SLOT, DEPTH)
        parts.append(jnp.where(live, rows.T, 0.0))
    both = dot3((lines[0], lines[1]), split(jnp.concatenate(parts, 0)))
    moved = both[: PLANES * ROWS] * phases[: PLANES * ROWS]
    moved = moved + both[PLANES * ROWS :] * phases[PLANES * ROWS :]
    send[:, 0:ROWS, :] = moved.reshape(PLANES, ROWS, 128)
    send[:, ROWS : ROWS + 1, :] = jnp.broadcast_to(ids[None], (PLANES, 1, 128))

    def outgoing(step):
        other = lax.rem(me + step, PLANES)
        return pltpu.make_async_remote_copy(
            src_ref=send.at[other],
            dst_ref=recv.at[step],
            send_sem=pl_send.at[step],
            recv_sem=pl_recv.at[step],
            device_id=(tg, other),
            device_id_type=MESH,
        )

    def launch(step, carry):
        outgoing(step).start()
        return carry

    lax.fori_loop(1, PLANES, launch, 0)
    recv[0] = send[me]

    column = lax.broadcasted_iota(jnp.int32, (2 * KEPT, 128), 0).astype(F32).astype(BF)
    second = jnp.where(lax.broadcasted_iota(jnp.int32, (16, 128), 0) >= 8, 1.0, 0.0).astype(F32)
    one, zero = jnp.ones((), BF), jnp.zeros((), BF)

    def place(g, carry):
        def arrive(i, carry):
            outgoing(g * STEP + i).wait_recv()
            return carry

        lax.fori_loop(jnp.where(g == 0, 1, 0), STEP, arrive, 0)
        block = recv[pl.ds(g * STEP, STEP)]
        left, right = [], []
        for i in range(STEP):
            high, low = split(block[i, 0:ROWS])
            row = block[i, ROWS : ROWS + 1]
            upper = jnp.floor(row * (1.0 / 256.0))
            lower = (row - 256.0 * upper).astype(BF)
            match = (upper - second).astype(BF)
            pieces = []
            for value in (high, low):
                value = jnp.concatenate([value, value], 0)
                for j in range(KEPT // 4):
                    pieces.append(jnp.where(match == jnp.asarray(2.0 * j, BF), value, zero))
            left.append(jnp.concatenate(pieces, 0))
            right.append(jnp.where(column == lower, one, zero))
        left = jnp.concatenate(left, 1)
        right = jnp.concatenate(right, 1)
        onehot[g] = right
        total = lax.dot_general(
            left, right, (((1,), (1,)), ((), ())), preferred_element_type=F32
        )
        half = KEPT // 2 * ROWS
        total = total[:half] + total[half:]

        @pl.when(g == 0)
        def _():
            spread[0] = total[:, :KEPT]
            spread[1] = total[:, KEPT:]

        @pl.when(g > 0)
        def _():
            spread[0] += total[:, :KEPT]
            spread[1] += total[:, KEPT:]

        return carry

    lax.fori_loop(0, PLANES // STEP, place, 0)

    corner = spread[0, 0:ROWS]
    lane = lax.broadcasted_iota(jnp.int32, (ROWS, 128), 1)
    edge_x = jnp.where(lane == 0, corner, 0.0).sum(axis=1, keepdims=True)
    edge_y = jnp.where(lane == 1, corner, 0.0).sum(axis=1, keepdims=True)
    spread[0, 0:ROWS] = jnp.where(lane < 2, 0.0, corner)
    fetches[3].wait()
    columns = []
    for z in range(LAYERS):
        stack = []
        for part in range(2):
            for parity in range(2):
                stack.append(spread[parity, pl.ds(part * LAYERS + z, KEPT // 2, stride=ROWS), :])
        columns.append(jnp.concatenate(stack, 0))
    mixed = dot3((ax[0], ax[1]), split(jnp.concatenate(columns, 1)))
    fields[...] = mixed

    fetches[4].wait()
    fetches[5].wait()
    fetches[6].wait()
    cos_x, sin_x = quarter(lax.broadcasted_iota(jnp.int32, (NG, KEPT), 0))
    cos_y, sin_y = quarter(lax.broadcasted_iota(jnp.int32, (1, NG), 1))
    row_id = lax.broadcasted_iota(jnp.int32, (ROWS, 128), 0)
    got_x = jnp.zeros((ROWS, 128), F32)
    got_y = jnp.zeros((ROWS, 128), F32)
    centre = lax.broadcasted_iota(jnp.int32, (1, KEPT), 1) == KEPT // 2
    for z in range(LAYERS):
        re = fields[0:NG, z * KEPT : (z + 1) * KEPT]
        im = fields[NG : 2 * NG, z * KEPT : (z + 1) * KEPT]
        er = jnp.where(centre, edge_x[z : z + 1], 0.0)
        ei = jnp.where(centre, edge_x[LAYERS + z : LAYERS + z + 1], 0.0)
        re = re + (cos_x * er - sin_x * ei)
        im = im + (sin_x * er + cos_x * ei)
        wave = dot3(split(jnp.concatenate([re, im], 1)), (ay[0], ay[1]))
        er = edge_y[z : z + 1]
        ei = edge_y[LAYERS + z : LAYERS + z + 1]
        local = pot[z]
        re = (wave[:, :NG] + (cos_y * er - sin_y * ei)) * local
        im = (wave[:, NG:] + (sin_y * er + cos_y * ei)) * local
        sum_re = re.sum(axis=0, keepdims=True)
        sum_im = im.sum(axis=0, keepdims=True)
        er = (cos_y * sum_re + sin_y * sum_im).sum(axis=1, keepdims=True)
        ei = (cos_y * sum_im - sin_y * sum_re).sum(axis=1, keepdims=True)
        got_y = jnp.where(row_id == z, er, jnp.where(row_id == LAYERS + z, ei, got_y))
        mid = dot3(split(jnp.concatenate([re, im], 1)), (ayt[0], ayt[1]))
        re, im = mid[:, :KEPT], mid[:, KEPT:]
        er = (cos_x * re + sin_x * im).sum(axis=0, keepdims=True)
        ei = (cos_x * im - sin_x * re).sum(axis=0, keepdims=True)
        er = jnp.where(centre, er, 0.0).sum(axis=1, keepdims=True)
        ei = jnp.where(centre, ei, 0.0).sum(axis=1, keepdims=True)
        got_x = jnp.where(row_id == z, er, jnp.where(row_id == LAYERS + z, ei, got_x))
        fields[0:NG, z * KEPT : (z + 1) * KEPT] = re
        fields[NG : 2 * NG, z * KEPT : (z + 1) * KEPT] = im
    fetches[7].wait()
    mixed = dot3((axt[0], axt[1]), split(fields[...]))
    for z in range(LAYERS):
        for part in range(2):
            block = mixed[part * KEPT : (part + 1) * KEPT, z * KEPT : (z + 1) * KEPT]
            for parity in range(2):
                plane[parity, pl.ds(part * LAYERS + z, KEPT // 2, stride=ROWS), :] = block[
                    parity * (KEPT // 2) : (parity + 1) * (KEPT // 2)
                ]
    corner = plane[0, 0:ROWS]
    plane[0, 0:ROWS] = jnp.where(lane == 0, got_x, jnp.where(lane == 1, got_y, corner))
    for parity in range(2):
        high, low = split(plane[parity])
        psi[:, parity * KEPT : (parity + 1) * KEPT] = high
        psi[:, (2 + parity) * KEPT : (3 + parity) * KEPT] = low

    def incoming(step):
        other = lax.rem(me - step + PLANES, PLANES)
        return pltpu.make_async_remote_copy(
            src_ref=sback.at[step],
            dst_ref=ret.at[me],
            send_sem=rt_send.at[step],
            recv_sem=rt_recv.at[step],
            device_id=(tg, other),
            device_id_type=MESH,
        )

    def pick(g, carry):
        for i in range(STEP):
            right = onehot[g, :, i * 128 : (i + 1) * 128]
            found = dot(psi[...], jnp.concatenate([right, right], 0))
            row = recv[g * STEP + i, ROWS : ROWS + 1]
            upper = jnp.broadcast_to(jnp.floor(row * (1.0 / 256.0)), (ROWS, 128))
            value = jnp.zeros((ROWS, 128), F32)
            for j in range(KEPT // 2):
                value = jnp.where(upper == float(j), found[j * ROWS : (j + 1) * ROWS], value)
            sback[g * STEP + i] = value

        def leave(i, carry):
            incoming(g * STEP + i).start()
            return carry

        lax.fori_loop(jnp.where(g == 0, 1, 0), STEP, leave, 0)
        return carry

    lax.fori_loop(0, PLANES // STEP, pick, 0)
    ret[me] = sback[0]

    def settle(step, carry):
        incoming(step).wait_recv()
        return carry

    lax.fori_loop(1, PLANES, settle, 0)
    fetches[8].wait()
    arrived = ret[...].reshape(PLANES * ROWS, 128)
    pair = jnp.concatenate(
        [arrived * phases[: PLANES * ROWS], arrived * phases[PLANES * ROWS :]], 0
    )
    picked = dot3((lines_t[0], lines_t[1]), split(pair))
    for part in range(2):
        rows = picked[part * DEPTH : (part + 1) * DEPTH].T
        back[part] = rows.reshape(GROUPS, SLOT, DEPTH)

    copies = []
    for step in range(1, GROUPS):
        other = lax.rem(tg + step, GROUPS)
        copy = pltpu.make_async_remote_copy(
            src_ref=back.at[:, other],
            dst_ref=result.at[:, tg],
            send_sem=out_send.at[step],
            recv_sem=out_recv.at[step],
            device_id=(other, me),
            device_id_type=MESH,
        )
        copy.start()
        copies.append(copy)
    own = pltpu.make_async_copy(back.at[:, tg], result.at[:, tg], local_sem.at[0])
    own.start()

    def finish(step, carry):
        outgoing(step).wait_send()
        incoming(step).wait_send()
        return carry

    lax.fori_loop(1, PLANES, finish, 0)
    own.wait()
    for copy in copies:
        copy.wait()


def apply_local(coeffs, meta, potential):
    consts = [jnp.asarray(t) for t in tables()]
    vmem = lambda *shape, dtype=F32: pltpu.VMEM(shape, dtype)
    dma = pltpu.SemaphoreType.DMA
    return pl.pallas_call(
        kernel,
        out_shape=jax.ShapeDtypeStruct((2, GROUPS, SLOT, DEPTH), F32),
        in_specs=[
            pl.BlockSpec(memory_space=pl.ANY),
            pl.BlockSpec(memory_space=pltpu.VMEM),
            pl.BlockSpec(memory_space=pl.ANY),
        ]
        + [pl.BlockSpec(memory_space=pl.ANY)] * len(consts),
        out_specs=pl.BlockSpec(memory_space=pltpu.VMEM),
        scratch_shapes=[
            vmem(2, GROUPS, SLOT, DEPTH),
            vmem(GROUPS, 8, 128),
            vmem(LAYERS, NG, NG),
        ]
        + [vmem(*t.shape, dtype=BF) for t in consts]
        + [
            vmem(PLANES, ROWS + 1, 128),
            vmem(PLANES, ROWS + 1, 128),
            vmem(2 * PLANES * ROWS, 128),
            vmem(PLANES // STEP, 2 * KEPT, STEP * 128, dtype=BF),
            vmem(2, KEPT // 2 * ROWS, KEPT),
            vmem(2, KEPT // 2 * ROWS, KEPT),
            vmem(KEPT // 2 * ROWS, 4 * KEPT, dtype=BF),
            vmem(2 * NG, LAYERS * KEPT),
            vmem(PLANES, ROWS, 128),
            vmem(PLANES, ROWS, 128),
            vmem(2, GROUPS, SLOT, DEPTH),
            dma((9,)),
            dma((GROUPS,)),
            dma((GROUPS,)),
            dma((GROUPS,)),
            dma((GROUPS,)),
            dma((GROUPS,)),
            dma((GROUPS,)),
            dma((PLANES,)),
            dma((PLANES,)),
            dma((PLANES,)),
            dma((PLANES,)),
        ],
        compiler_params=pltpu.CompilerParams(
            collective_id=0, has_side_effects=True, vmem_limit_bytes=48 * 1024 * 1024
        ),
    )(coeffs, meta, potential, *consts)


def signed(index):
    return jnp.where(index < NG // 2, index, index - NG)


def local(coeffs, potential, stick_x, stick_y, stick_count, stick_offset):
    lane = jnp.arange(128, dtype=jnp.int32)
    mine = lane // SLOT == lax.axis_index("tg")
    freq_x, freq_y = signed(stick_x), signed(stick_y)
    cell_x, cell_y = freq_x + KEPT // 2, freq_y + KEPT // 2
    ids = (cell_x // 2) * 256 + (cell_x % 2) * 128 + cell_y
    ids = jnp.where(freq_x == KEPT // 2, 0, jnp.where(freq_y == KEPT // 2, 1, ids))
    ids = jnp.where(stick_count > 0, ids, -256)
    rows = lax.broadcasted_iota(jnp.int32, (8, 128), 0)
    wide = lambda v: jnp.where(mine, jnp.tile(v, GROUPS), 0)[None]
    meta = jnp.where(
        rows == 0,
        wide(ids),
        jnp.where(rows == 1, wide(stick_count), jnp.where(rows == 2, wide(stick_offset), 0)),
    ).astype(F32)
    picked = apply_local(coeffs, meta, potential)
    depth_ids = jnp.arange(DEPTH, dtype=jnp.int32)
    live = depth_ids[None, :] < stick_count[:, None]
    z_index = (stick_offset[:, None] + depth_ids[None, :]) % NG
    squared = (freq_x**2 + freq_y**2)[:, None] + signed(z_index) ** 2
    kinetic = 0.5 * (32.0 / (NG * NG)) * squared.astype(F32)
    return jnp.where(live, picked + kinetic * coeffs, 0.0)


def solution(mesh):
    in_specs = (
        P(None, None, ("tg", "pl"), None),
        P("pl", None, None),
        P(("tg", "pl")),
        P(("tg", "pl")),
        P(("tg", "pl")),
        P(("tg", "pl")),
    )
    out_specs = P(None, None, ("tg", "pl"), None)
    return jax.shard_map(local, mesh=mesh, in_specs=in_specs, out_specs=out_specs, check_vma=False)
```

profile of v0, /device:TPU:1, one launch (start us, length us, event | category | flops | bytes accessed | tf_op | source)
XLA Modules:
  0.0 68.7 jit_solution(11576368869852062248)
XLA Ops:
  0.0 0.0 copy-start.8
  0.0 0.7 copy-done.8
  0.7 0.0 copy-start.9
  0.7 0.1 tile.30
  0.7 0.6 copy-done.9
  1.3 0.1 tile.32
  1.4 0.0 copy-start.10
  1.4 0.0 copy-start.11
  1.4 0.6 copy-done.10
  2.1 0.0 copy-done.11
  2.1 0.1 tile.13
  2.2 0.1 select_convert_fusion.meta
  2.3 0.0 copy-start
  2.3 1.2 %copy-done = f32[4,256,256]{2,1,0:T(8,128)S(1)} copy-done((f32[4,256,256]{2,1,0:T(8,128)S(1)}, f32[4,256,256]{2,1,0:T(8,128)}, u32[]{:S(2)}) %copy-start) | copy-done | bytes 1048600
  3.5 0.0 copy-start.1
  3.5 1.2 %copy-done.1 = bf16[2,1024,256]{2,1,0:T(8,128)(2,1)S(1)} copy-done((bf16[2,1024,256]{2,1,0:T(8,128)(2,1)S(1)}, bf16[2,1024,256]{2,1,0:T(8,128)(2,1)}, u32[]{:S(2)}) %copy-start.1) | copy-done | bytes 1048600
  4.7 0.0 copy-start.2
  4.7 1.2 %copy-done.2 = bf16[2,256,1024]{2,1,0:T(8,128)(2,1)S(1)} copy-done((bf16[2,256,1024]{2,1,0:T(8,128)(2,1)S(1)}, bf16[2,256,1024]{2,1,0:T(8,128)(2,1)}, u32[]{:S(2)}) %copy-start.2) | copy-done | bytes 1048600
  6.0 0.0 copy-start.3
  6.0 0.9 %copy-done.3 = f32[2,4,32,128]{3,2,1,0:T(8,128)S(1)} copy-done((f32[2,4,32,128]{3,2,1,0:T(8,128)S(1)}, f32[2,4,32,128]{3,2,1,0:T(8,128)}, u32[]{:S(2)}) %copy-start.3) | copy-done | bytes 131096
  6.9 0.0 copy-start.4
  6.9 1.0 %copy-done.4 = bf16[2,512,256]{2,1,0:T(8,128)(2,1)S(1)} copy-done((bf16[2,512,256]{2,1,0:T(8,128)(2,1)S(1)}, bf16[2,512,256]{2,1,0:T(8,128)(2,1)}, u32[]{:S(2)}) %copy-start.4) | copy-done | bytes 524312
  7.9 0.0 copy-start.5
  7.9 1.0 %copy-done.5 = bf16[2,256,512]{2,1,0:T(8,128)(2,1)S(1)} copy-done((bf16[2,256,512]{2,1,0:T(8,128)(2,1)S(1)}, bf16[2,256,512]{2,1,0:T(8,128)(2,1)}, u32[]{:S(2)}) %copy-start.5) | copy-done | bytes 524312
  9.0 0.0 copy-start.6
  9.0 1.0 %copy-done.6 = bf16[2,256,512]{2,1,0:T(8,128)(2,1)S(1)} copy-done((bf16[2,256,512]{2,1,0:T(8,128)(2,1)S(1)}, bf16[2,256,512]{2,1,0:T(8,128)(2,1)}, u32[]{:S(2)}) %copy-start.6) | copy-done | bytes 524312
  10.0 0.0 copy-start.7
  10.0 1.0 %copy-done.7 = bf16[2,512,256]{2,1,0:T(8,128)(2,1)S(1)} copy-done((bf16[2,512,256]{2,1,0:T(8,128)(2,1)S(1)}, bf16[2,512,256]{2,1,0:T(8,128)(2,1)}, u32[]{:S(2)}) %copy-start.7) | copy-done | bytes 524312
  11.0 56.8 %shard_map.127 = f32[2,4,32,128]{3,2,1,0:T(8,128)S(1)} custom-call(f32[2,4,32,128]{3,2,1,0:T(8,128)S(1)} %copy-done.3, f32[8,128]{1,0:T(8,128)S(1)} %select_convert_fusion.meta, f32[4,256,256]{2,1,0:T(8,128)S(1)} %copy-done, bf16[2,1024,256]{2,1,0:T(8,128)(2,1)S(1)} %copy-done.1, bf16[2,256,1024]{2,1,0:T(8,128)(2,1)S(1)} %copy-done.2, ...), custom_call_target="tpu_custom_call" | custom-call | tf_op jit(solution)/shard_map/pallas_call | solution.py:421
  67.9 0.1 fusion.4
  68.0 0.1 iota_compare_fusion
  68.1 0.7 add_select_fusion
  (8 shorter events, 0.1 us)
Async XLA Ops:
  0.0 0.7 copy-start.8
  0.7 0.7 copy-start.9
  1.4 0.7 copy-start.10
  1.4 0.7 copy-start.11
  2.3 1.2 %copy-start = (f32[4,256,256]{2,1,0:T(8,128)S(1)}, f32[4,256,256]{2,1,0:T(8,128)}, u32[]{:S(2)}) copy-start(f32[4,256,256]{2,1,0:T(8,128)} %potential.1) | copy-start | bytes 3145732
  3.5 1.2 %copy-start.1 = (bf16[2,1024,256]{2,1,0:T(8,128)(2,1)S(1)}, bf16[2,1024,256]{2,1,0:T(8,128)(2,1)}, u32[]{:S(2)}) copy-start(bf16[2,1024,256]{2,1,0:T(8,128)(2,1)} %constant.101.clone.lines_hbm) | copy-start | bytes 3145732
  4.7 1.2 %copy-start.2 = (bf16[2,256,1024]{2,1,0:T(8,128)(2,1)S(1)}, bf16[2,256,1024]{2,1,0:T(8,128)(2,1)}, u32[]{:S(2)}) copy-start(bf16[2,256,1024]{2,1,0:T(8,128)(2,1)} %constant.102.clone.lines_t_hbm) | copy-start | bytes 3145732
  6.0 0.9 %copy-start.3 = (f32[2,4,32,128]{3,2,1,0:T(8,128)S(1)}, f32[2,4,32,128]{3,2,1,0:T(8,128)}, u32[]{:S(2)}) copy-start(f32[2,4,32,128]{3,2,1,0:T(8,128)} %coeffs.1) | copy-start | bytes 393220
  6.9 1.0 %copy-start.4 = (bf16[2,512,256]{2,1,0:T(8,128)(2,1)S(1)}, bf16[2,512,256]{2,1,0:T(8,128)(2,1)}, u32[]{:S(2)}) copy-start(bf16[2,512,256]{2,1,0:T(8,128)(2,1)} %constant.104.clone.ax_hbm) | copy-start | bytes 1572868
  7.9 1.0 %copy-start.5 = (bf16[2,256,512]{2,1,0:T(8,128)(2,1)S(1)}, bf16[2,256,512]{2,1,0:T(8,128)(2,1)}, u32[]{:S(2)}) copy-start(bf16[2,256,512]{2,1,0:T(8,128)(2,1)} %constant.105.clone.axt_hbm) | copy-start | bytes 1572868
  9.0 1.0 %copy-start.6 = (bf16[2,256,512]{2,1,0:T(8,128)(2,1)S(1)}, bf16[2,256,512]{2,1,0:T(8,128)(2,1)}, u32[]{:S(2)}) copy-start(bf16[2,256,512]{2,1,0:T(8,128)(2,1)} %constant.106.clone.ay_hbm) | copy-start | bytes 1572868
  10.0 1.0 %copy-start.7 = (bf16[2,512,256]{2,1,0:T(8,128)(2,1)S(1)}, bf16[2,512,256]{2,1,0:T(8,128)(2,1)}, u32[]{:S(2)}) copy-start(bf16[2,512,256]{2,1,0:T(8,128)(2,1)} %constant.107.clone.ayt_hbm) | copy-start | bytes 1572868
where the time goes:
time: 69.2 us; the launch traced here: 68.7 us
  Pallas kernels  56.8 us (82%)
  local copies, waits for them, and re-layouts  10.9 us (16%)
  other arithmetic  0.96 us (1%)
    pallas_call x1, Pallas kernels, apply_local(): pl.pallas_call(kernel, out_shape=jax.ShapeDtypeStruct((2, GROUPS, SLOT, D...  56.8 us
    unnamed x24, local copies, waits for them, and re-layouts  10.6 us

commit v1 on v0

--- a/solution.py
+++ b/solution.py
@@ -76,6 +76,14 @@
     return dot(a[0], b[0]) + (dot(a[0], b[1]) + dot(a[1], b[0]))
 
 
+def settle(ref, semaphore):
+    pltpu.make_async_copy(ref, ref, semaphore).wait()
+
+
+def signed(index):
+    return jnp.where(index < NG // 2, index, index - NG)
+
+
 def quarter(index):
     index = index & 3
     one, zero = jnp.float32(1.0), jnp.float32(0.0)
@@ -86,8 +94,11 @@
 
 def kernel(
     coeffs,
-    meta,
     potential,
+    stick_x,
+    stick_y,
+    stick_count,
+    stick_offset,
     lines_hbm,
     lines_t_hbm,
     phase_hbm,
@@ -97,6 +108,9 @@
     ayt_hbm,
     result,
     group,
+    coef,
+    sticks,
+    meta,
     metas,
     pot,
     lines,
@@ -117,6 +131,8 @@
     sback,
     ret,
     back,
+    picks,
+    stick_sem,
     local_sem,
     tg_send,
     tg_recv,
@@ -144,33 +160,56 @@
                 (ayt_hbm, ayt),
                 (axt_hbm, axt),
                 (lines_t_hbm, lines_t),
+                (coeffs, coef),
             ]
         )
     ]
-    for fetch in fetches:
+    rows = [
+        pltpu.make_async_copy(src, sticks.at[i], stick_sem.at[i])
+        for i, src in enumerate((stick_x, stick_y, stick_count, stick_offset))
+    ]
+    for fetch in rows + fetches[9:] + fetches[:9]:
         fetch.start()
 
     barrier = pltpu.get_barrier_semaphore()
     for step in range(1, GROUPS):
         pl.semaphore_signal(
-            barrier, inc=1, device_id=(lax.rem(tg + step, GROUPS), me), device_id_type=MESH
+            barrier, inc=1, device_id=((tg + step) & (GROUPS - 1), me), device_id_type=MESH
         )
 
     def greet(step, carry):
         pl.semaphore_signal(
-            barrier, inc=1, device_id=(tg, lax.rem(me + step, PLANES)), device_id_type=MESH
+            barrier, inc=1, device_id=(tg, (me + step) & (PLANES - 1)), device_id_type=MESH
         )
         return carry
 
-    lax.fori_loop(1, PLANES, greet, 0)
+    lax.fori_loop(1, PLANES, greet, 0, unroll=True)
+    for row in rows:
+        row.wait()
+    mine = sticks[...]
+    mine = jnp.concatenate([mine] * GROUPS, 1)
+    index_x, index_y, counts, offsets = mine[0:1], mine[1:2], mine[2:3], mine[3:4]
+    freq_x, freq_y = signed(index_x), signed(index_y)
+    cell_x, cell_y = freq_x + KEPT // 2, freq_y + KEPT // 2
+    cells = (cell_x >> 1) * 256 + (cell_x & 1) * 128 + cell_y
+    cells = jnp.where(freq_x == KEPT // 2, 0, jnp.where(freq_y == KEPT // 2, 1, cells))
+    cells = jnp.where(counts > 0, cells, -256)
+    row_id = lax.broadcasted_iota(jnp.int32, (ROWS, 128), 0)
+    own = jnp.where(row_id == 3, freq_x * freq_x + freq_y * freq_y, 0)
+    own = jnp.where(row_id == 2, offsets, jnp.where(row_id == 1, counts, own))
+    own = jnp.where(row_id == 0, cells, own).astype(F32)
+    owner = lax.broadcasted_iota(jnp.int32, (ROWS, 128), 1) // SLOT
+    meta[...] = own
     pl.semaphore_wait(barrier, GROUPS - 1 + PLANES - 1)
 
+    fetches[9].wait()
+
     copies = []
-    for step in range(1, GROUPS):
-        other = lax.rem(tg + step, GROUPS)
+    for step in (2, 1, 3):
+        other = (tg + step) & (GROUPS - 1)
         for src, dst, sems in (
             (meta, metas.at[step], (meta_send, meta_recv)),
-            (coeffs.at[:, other], group.at[:, tg], (tg_send, tg_recv)),
+            (coef.at[:, other], group.at[:, tg], (tg_send, tg_recv)),
         ):
             copy = pltpu.make_async_remote_copy(
                 src_ref=src,
@@ -184,7 +223,9 @@
             copies.append(copy)
     for copy in copies[0::2]:
         copy.wait()
-    info = meta[...] + metas[1] + metas[2] + metas[3]
+    info = own
+    for step in range(1, GROUPS):
+        info = jnp.where(owner == (tg - step) & (GROUPS - 1), metas[step], info)
     ids, count, offset = info[0:1], info[1:2], info[2:3]
     fetches[1].wait()
     steps = lax.broadcasted_iota(jnp.int32, (NG, 128), 0).astype(F32)
@@ -206,22 +247,26 @@
     send[:, 0:ROWS, :] = moved.reshape(PLANES, ROWS, 128)
     send[:, ROWS : ROWS + 1, :] = jnp.broadcast_to(ids[None], (PLANES, 1, 128))
 
-    def outgoing(step):
-        other = lax.rem(me + step, PLANES)
+    def peer(ring, spot, sign):
+        along_z = ((ring + 1) >> 1) * (2 * (ring & 1) - 1)
+        x = ((me >> 4) + sign * (spot >> 1)) & 3
+        z = ((me >> 1) + sign * along_z) & 7
+        return x * 16 + z * 2 + ((me + spot) & 1)
+
+    def outgoing(ring, spot):
+        other = peer(ring, spot, 1)
         return pltpu.make_async_remote_copy(
             src_ref=send.at[other],
-            dst_ref=recv.at[step],
-            send_sem=pl_send.at[step],
-            recv_sem=pl_recv.at[step],
+            dst_ref=recv.at[ring * STEP + spot],
+            send_sem=pl_send.at[0],
+            recv_sem=pl_recv.at[ring],
             device_id=(tg, other),
             device_id_type=MESH,
         )
 
-    def launch(step, carry):
-        outgoing(step).start()
-        return carry
-
-    lax.fori_loop(1, PLANES, launch, 0)
+    for ring in range(PLANES // STEP):
+        for spot in range(0 if ring else 1, STEP):
+            outgoing(ring, spot).start()
     recv[0] = send[me]
 
     column = lax.broadcasted_iota(jnp.int32, (2 * KEPT, 128), 0).astype(F32).astype(BF)
@@ -229,11 +274,14 @@
     one, zero = jnp.ones((), BF), jnp.zeros((), BF)
 
     def place(g, carry):
-        def arrive(i, carry):
-            outgoing(g * STEP + i).wait_recv()
-            return carry
-
-        lax.fori_loop(jnp.where(g == 0, 1, 0), STEP, arrive, 0)
+        @pl.when(g == 0)
+        def _():
+            settle(recv.at[pl.ds(1, STEP - 1)], pl_recv.at[0])
+
+        @pl.when(g > 0)
+        def _():
+            settle(recv.at[pl.ds(g * STEP, STEP)], pl_recv.at[g])
+
         block = recv[pl.ds(g * STEP, STEP)]
         left, right = [], []
         for i in range(STEP):
@@ -293,7 +341,6 @@
     fetches[6].wait()
     cos_x, sin_x = quarter(lax.broadcasted_iota(jnp.int32, (NG, KEPT), 0))
     cos_y, sin_y = quarter(lax.broadcasted_iota(jnp.int32, (1, NG), 1))
-    row_id = lax.broadcasted_iota(jnp.int32, (ROWS, 128), 0)
     got_x = jnp.zeros((ROWS, 128), F32)
     got_y = jnp.zeros((ROWS, 128), F32)
     centre = lax.broadcasted_iota(jnp.int32, (1, KEPT), 1) == KEPT // 2
@@ -340,43 +387,47 @@
         psi[:, parity * KEPT : (parity + 1) * KEPT] = high
         psi[:, (2 + parity) * KEPT : (3 + parity) * KEPT] = low
 
-    def incoming(step):
-        other = lax.rem(me - step + PLANES, PLANES)
+    def incoming(ring, spot):
+        other = peer(ring, spot, -1)
         return pltpu.make_async_remote_copy(
-            src_ref=sback.at[step],
+            src_ref=sback.at[ring * STEP + spot],
             dst_ref=ret.at[me],
-            send_sem=rt_send.at[step],
-            recv_sem=rt_recv.at[step],
+            send_sem=rt_send.at[0],
+            recv_sem=rt_recv.at[0],
             device_id=(tg, other),
             device_id_type=MESH,
         )
 
-    def pick(g, carry):
-        for i in range(STEP):
-            right = onehot[g, :, i * 128 : (i + 1) * 128]
+    def pick(turn, carry):
+        g = PLANES // STEP - 1 - turn
+        for i in range(0, STEP, 2):
+            right = onehot[g, :, i * 128 : (i + 2) * 128]
             found = dot(psi[...], jnp.concatenate([right, right], 0))
-            row = recv[g * STEP + i, ROWS : ROWS + 1]
-            upper = jnp.broadcast_to(jnp.floor(row * (1.0 / 256.0)), (ROWS, 128))
-            value = jnp.zeros((ROWS, 128), F32)
+            row = jnp.concatenate(
+                [recv[g * STEP + i + e, ROWS : ROWS + 1] for e in range(2)], 1
+            )
+            upper = jnp.broadcast_to(jnp.floor(row * (1.0 / 256.0)), (ROWS, 256))
+            value = jnp.zeros((ROWS, 256), F32)
             for j in range(KEPT // 2):
                 value = jnp.where(upper == float(j), found[j * ROWS : (j + 1) * ROWS], value)
-            sback[g * STEP + i] = value
-
-        def leave(i, carry):
-            incoming(g * STEP + i).start()
-            return carry
-
-        lax.fori_loop(jnp.where(g == 0, 1, 0), STEP, leave, 0)
+            for e in range(2):
+                sback[g * STEP + i + e] = value[:, e * 128 : (e + 1) * 128]
+
+        for i in range(STEP):
+            if i > 0:
+                incoming(g, i).start()
+            else:
+
+                @pl.when(g > 0)
+                def _():
+                    incoming(g, 0).start()
+
         return carry
 
     lax.fori_loop(0, PLANES // STEP, pick, 0)
     ret[me] = sback[0]
 
-    def settle(step, carry):
-        incoming(step).wait_recv()
-        return carry
-
-    lax.fori_loop(1, PLANES, settle, 0)
+    settle(ret.at[pl.ds(1, PLANES - 1)], rt_recv.at[0])
     fetches[8].wait()
     arrived = ret[...].reshape(PLANES * ROWS, 128)
     pair = jnp.concatenate(
@@ -388,11 +439,11 @@
         back[part] = rows.reshape(GROUPS, SLOT, DEPTH)
 
     copies = []
-    for step in range(1, GROUPS):
-        other = lax.rem(tg + step, GROUPS)
+    for step in (2, 1, 3):
+        other = (tg + step) & (GROUPS - 1)
         copy = pltpu.make_async_remote_copy(
             src_ref=back.at[:, other],
-            dst_ref=result.at[:, tg],
+            dst_ref=picks.at[:, tg],
             send_sem=out_send.at[step],
             recv_sem=out_recv.at[step],
             device_id=(other, me),
@@ -400,36 +451,43 @@
         )
         copy.start()
         copies.append(copy)
-    own = pltpu.make_async_copy(back.at[:, tg], result.at[:, tg], local_sem.at[0])
-    own.start()
-
-    def finish(step, carry):
-        outgoing(step).wait_send()
-        incoming(step).wait_send()
-        return carry
-
-    lax.fori_loop(1, PLANES, finish, 0)
-    own.wait()
-    for copy in copies:
+    column = own.T[:SLOT]
+    position = lax.broadcasted_iota(jnp.int32, (SLOT, DEPTH), 1).astype(F32)
+    live = position < column[:, 1:2]
+    height = position + column[:, 2:3]
+    height = jnp.where(height >= float(NG), height - float(NG), height)
+    height = jnp.where(height >= float(NG // 2), height - float(NG), height)
+    kinetic = (0.5 * (32.0 / (NG * NG))) * (column[:, 3:4] + height * height)
+    def add(band, value):
+        for part in range(2):
+            term = kinetic * coef[part, band]
+            result[part, band] = jnp.where(live, value[part] + term, 0.0)
+
+    add(tg, [back[0, tg], back[1, tg]])
+
+    settle(send.at[pl.ds(1, PLANES - 1)], pl_send.at[0])
+    settle(sback.at[pl.ds(1, PLANES - 1)], rt_send.at[0])
+    for step, copy in zip((1, 3, 2), copies[1:] + copies[:1]):
         copy.wait()
-
-
-def apply_local(coeffs, meta, potential):
+        band = (tg - step) & (GROUPS - 1)
+        add(band, [picks[0, band], picks[1, band]])
+
+
+def local(coeffs, potential, stick_x, stick_y, stick_count, stick_offset):
     consts = [jnp.asarray(t) for t in tables()]
     vmem = lambda *shape, dtype=F32: pltpu.VMEM(shape, dtype)
     dma = pltpu.SemaphoreType.DMA
+    args = (coeffs, potential, stick_x, stick_y, stick_count, stick_offset, *consts)
     return pl.pallas_call(
         kernel,
         out_shape=jax.ShapeDtypeStruct((2, GROUPS, SLOT, DEPTH), F32),
-        in_specs=[
-            pl.BlockSpec(memory_space=pl.ANY),
-            pl.BlockSpec(memory_space=pltpu.VMEM),
-            pl.BlockSpec(memory_space=pl.ANY),
-        ]
-        + [pl.BlockSpec(memory_space=pl.ANY)] * len(consts),
+        in_specs=[pl.BlockSpec(memory_space=pltpu.HBM)] * len(args),
         out_specs=pl.BlockSpec(memory_space=pltpu.VMEM),
         scratch_shapes=[
             vmem(2, GROUPS, SLOT, DEPTH),
+            vmem(2, GROUPS, SLOT, DEPTH),
+            vmem(4, SLOT, dtype=jnp.int32),
+            vmem(8, 128),
             vmem(GROUPS, 8, 128),
             vmem(LAYERS, NG, NG),
         ]
@@ -446,50 +504,16 @@
             vmem(PLANES, ROWS, 128),
             vmem(PLANES, ROWS, 128),
             vmem(2, GROUPS, SLOT, DEPTH),
-            dma((9,)),
-            dma((GROUPS,)),
-            dma((GROUPS,)),
-            dma((GROUPS,)),
-            dma((GROUPS,)),
-            dma((GROUPS,)),
-            dma((GROUPS,)),
-            dma((PLANES,)),
-            dma((PLANES,)),
-            dma((PLANES,)),
-            dma((PLANES,)),
-        ],
+            vmem(2, GROUPS, SLOT, DEPTH),
+            dma((4,)),
+            dma((10,)),
+        ]
+        + [dma((GROUPS,))] * 6
+        + [dma((1,)), dma((PLANES // STEP,)), dma((1,)), dma((1,))],
         compiler_params=pltpu.CompilerParams(
-            collective_id=0, has_side_effects=True, vmem_limit_bytes=48 * 1024 * 1024
+            collective_id=0, has_side_effects=True, vmem_limit_bytes=62 * 1024 * 1024
         ),
-    )(coeffs, meta, potential, *consts)
-
-
-def signed(index):
-    return jnp.where(index < NG // 2, index, index - NG)
-
-
-def local(coeffs, potential, stick_x, stick_y, stick_count, stick_offset):
-    lane = jnp.arange(128, dtype=jnp.int32)
-    mine = lane // SLOT == lax.axis_index("tg")
-    freq_x, freq_y = signed(stick_x), signed(stick_y)
-    cell_x, cell_y = freq_x + KEPT // 2, freq_y + KEPT // 2
-    ids = (cell_x // 2) * 256 + (cell_x % 2) * 128 + cell_y
-    ids = jnp.where(freq_x == KEPT // 2, 0, jnp.where(freq_y == KEPT // 2, 1, ids))
-    ids = jnp.where(stick_count > 0, ids, -256)
-    rows = lax.broadcasted_iota(jnp.int32, (8, 128), 0)
-    wide = lambda v: jnp.where(mine, jnp.tile(v, GROUPS), 0)[None]
-    meta = jnp.where(
-        rows == 0,
-        wide(ids),
-        jnp.where(rows == 1, wide(stick_count), jnp.where(rows == 2, wide(stick_offset), 0)),
-    ).astype(F32)
-    picked = apply_local(coeffs, meta, potential)
-    depth_ids = jnp.arange(DEPTH, dtype=jnp.int32)
-    live = depth_ids[None, :] < stick_count[:, None]
-    z_index = (stick_offset[:, None] + depth_ids[None, :]) % NG
-    squared = (freq_x**2 + freq_y**2)[:, None] + signed(z_index) ** 2
-    kinetic = 0.5 * (32.0 / (NG * NG)) * squared.astype(F32)
-    return jnp.where(live, picked + kinetic * coeffs, 0.0)
+    )(*args)
 
 
 def solution(mesh):

time: 69.2 us -> 49.4 us (0.71)
  local copies, waits for them, and re-layouts: 10.9 us -> 1.57 us
  Pallas kernels: 56.8 us -> 47.7 us
  other arithmetic: 0.96 us -> 0 us
    pallas_call x1, Pallas kernels: 56.8 us -> 47.7 us  [local(): pl.pallas_call(kernel, out_shape=jax.ShapeDtypeStruct((2, GROUPS, SLOT, D...]
    unnamed x24 -> x1, local copies, waits for them, and re-layouts: 10.6 us -> 1.57 us
    select_n x3 -> x0, other arithmetic: 0.7 us -> none  [the longest x1 0.69 us: local(): return jnp.where(live, picked + kinetic * coeffs, 0.0)]
where the time goes in v1:
time: 49.4 us; the launch traced here: 49.3 us
  Pallas kernels  47.7 us (97%)
  local copies, waits for them, and re-layouts  1.57 us (3%)
    pallas_call x1, Pallas kernels, local(): pl.pallas_call(kernel, out_shape=jax.ShapeDtypeStruct((2, GROUPS, SLOT, D...  47.7 us
    unnamed x1, local copies, waits for them, and re-layouts  1.57 us

profile of v1, /device:TPU:1, one launch (start us, length us, event | category | flops | bytes accessed | tf_op | source)
XLA Modules:
  0.0 49.3 jit_solution(3971286747755378137)
XLA Ops:
  0.0 47.7 %shard_map.127 = f32[2,4,32,128]{3,2,1,0:T(8,128)} custom-call(f32[2,4,32,128]{3,2,1,0:T(8,128)} %coeffs.1, f32[4,256,256]{2,1,0:T(8,128)} %potential.1, s32[32]{0:T(128)} %stick_x.1, s32[32]{0:T(128)} %stick_y.1, s32[32]{0:T(128)} %stick_count.1, s32[32]{0:T(128)} %stick_offset.1, bf16[2,1024,256]{2,1,0:T(8,128)(2,1)} %constant.14.clone.lines_hbm, ...), custom_call_target="tpu_custom_call" | custom-call | tf_op jit(solution)/shard_map/pallas_call | solution.py:481
  47.8 1.6 %copy.15 = f32[2,4,32,128]{3,2,1,0:T(8,128)} copy(f32[2,4,32,128]{3,2,1,0:T(8,128)} %shard_map.127) | data formatting | bytes 262144

commit v2 on v1

--- a/solution.py
+++ b/solution.py
@@ -21,6 +21,9 @@
 LAYERS = 4
 ROWS = 2 * LAYERS
 KEPT = 128
+MAIN = 20
+LANES = GROUPS * MAIN + SLOT - MAIN
+PART = 32
 STEP = 8
 
 
@@ -72,8 +75,15 @@
     return jnp.dot(a, b, preferred_element_type=F32)
 
 
+def pack(values, chosen):
+    high, low = split(values)
+    return dot(high, chosen) + dot(low, chosen)
+
+
 def dot3(a, b):
-    return dot(a[0], b[0]) + (dot(a[0], b[1]) + dot(a[1], b[0]))
+    return dot(
+        jnp.concatenate([a[0], a[0], a[1]], 1), jnp.concatenate([b[0], b[1], b[0]], 0)
+    )
 
 
 def settle(ref, semaphore):
@@ -131,7 +141,8 @@
     sback,
     ret,
     back,
-    picks,
+    uppers,
+    terms,
     stick_sem,
     local_sem,
     tg_send,
@@ -193,16 +204,28 @@
     cell_x, cell_y = freq_x + KEPT // 2, freq_y + KEPT // 2
     cells = (cell_x >> 1) * 256 + (cell_x & 1) * 128 + cell_y
     cells = jnp.where(freq_x == KEPT // 2, 0, jnp.where(freq_y == KEPT // 2, 1, cells))
-    cells = jnp.where(counts > 0, cells, -256)
+    cells = jnp.where(counts > 0, cells + 1, 0)
+    offsets = jnp.where(counts > 0, offsets, 0)
     row_id = lax.broadcasted_iota(jnp.int32, (ROWS, 128), 0)
-    own = jnp.where(row_id == 3, freq_x * freq_x + freq_y * freq_y, 0)
-    own = jnp.where(row_id == 2, offsets, jnp.where(row_id == 1, counts, own))
-    own = jnp.where(row_id == 0, cells, own).astype(F32)
+    mine = jnp.where(row_id == 3, freq_x * freq_x + freq_y * freq_y, 0)
+    mine = jnp.where(row_id == 2, offsets, jnp.where(row_id == 1, counts, mine))
+    mine = jnp.where(row_id == 0, cells, mine).astype(F32)
     owner = lax.broadcasted_iota(jnp.int32, (ROWS, 128), 1) // SLOT
-    meta[...] = own
+    meta[...] = mine
     pl.semaphore_wait(barrier, GROUPS - 1 + PLANES - 1)
 
     fetches[9].wait()
+
+    def packing(slot, lane):
+        spot = slot & (SLOT - 1)
+        place = jnp.where(
+            spot < MAIN, (slot // SLOT) * MAIN + spot, spot + (GROUPS - 1) * MAIN
+        )
+        return jnp.where(place == lane, 1.0, 0.0).astype(BF)
+
+    along = lax.broadcasted_iota(jnp.int32, (128, 128), 0)
+    across = lax.broadcasted_iota(jnp.int32, (128, 128), 1)
+    pack_to, pack_from = packing(along, across), packing(across, along)
 
     copies = []
     for step in (2, 1, 3):
@@ -223,10 +246,12 @@
             copies.append(copy)
     for copy in copies[0::2]:
         copy.wait()
-    info = own
+    info = mine
     for step in range(1, GROUPS):
         info = jnp.where(owner == (tg - step) & (GROUPS - 1), metas[step], info)
-    ids, count, offset = info[0:1], info[1:2], info[2:3]
+    count = info[1:2]
+    packed = pack(info, pack_to)
+    ids, offset = packed[0:1] - 1.0, packed[2:3]
     fetches[1].wait()
     steps = lax.broadcasted_iota(jnp.int32, (NG, 128), 0).astype(F32)
     chosen = jnp.where(steps == offset, 1.0, 0.0).astype(BF)
@@ -241,7 +266,10 @@
     for part in range(2):
         rows = group[part].reshape(GROUPS * SLOT, DEPTH)
         parts.append(jnp.where(live, rows.T, 0.0))
-    both = dot3((lines[0], lines[1]), split(jnp.concatenate(parts, 0)))
+    masked = jnp.concatenate(parts, 0)
+    high, low = split(masked)
+    high, low = dot(high, pack_to).astype(BF), dot(low, pack_to).astype(BF)
+    both = dot3((lines[0], lines[1]), (high, low))
     moved = both[: PLANES * ROWS] * phases[: PLANES * ROWS]
     moved = moved + both[PLANES * ROWS :] * phases[PLANES * ROWS :]
     send[:, 0:ROWS, :] = moved.reshape(PLANES, ROWS, 128)
@@ -269,9 +297,17 @@
             outgoing(ring, spot).start()
     recv[0] = send[me]
 
+    height = steps[:DEPTH] + info[2:3]
+    height = jnp.where(height >= float(NG), height - float(NG), height)
+    height = jnp.where(height >= float(NG // 2), height - float(NG), height)
+    kinetic = (0.5 * (32.0 / (NG * NG))) * (info[3:4] + height * height)
+    terms[...] = jnp.concatenate([kinetic, kinetic], 0) * masked
+
     column = lax.broadcasted_iota(jnp.int32, (2 * KEPT, 128), 0).astype(F32).astype(BF)
     second = jnp.where(lax.broadcasted_iota(jnp.int32, (16, 128), 0) >= 8, 1.0, 0.0).astype(F32)
     one, zero = jnp.ones((), BF), jnp.zeros((), BF)
+
+    lane9 = lax.broadcasted_iota(jnp.int32, (ROWS + 1, 128), 1)
 
     def place(g, carry):
         @pl.when(g == 0)
@@ -284,11 +320,17 @@
 
         block = recv[pl.ds(g * STEP, STEP)]
         left, right = [], []
-        for i in range(STEP):
-            high, low = split(block[i, 0:ROWS])
-            row = block[i, ROWS : ROWS + 1]
+        tiles = []
+        for i in range(0, STEP, 4):
+            for t in range(3):
+                spread_out = pltpu.roll(block[i + 3], 96 - PART * t, 1)
+                tiles.append(jnp.where(lane9 < 96, block[i + t], spread_out))
+        for i, tile in enumerate(tiles):
+            high, low = split(tile[0:ROWS])
+            row = tile[ROWS : ROWS + 1]
             upper = jnp.floor(row * (1.0 / 256.0))
             lower = (row - 256.0 * upper).astype(BF)
+            uppers[g * len(tiles) + i] = jnp.broadcast_to(upper, (ROWS, 128))
             match = (upper - second).astype(BF)
             pieces = []
             for value in (high, low):
@@ -400,19 +442,25 @@
 
     def pick(turn, carry):
         g = PLANES // STEP - 1 - turn
-        for i in range(0, STEP, 2):
+        tiles = []
+        for i in range(0, STEP * 3 // 4, 2):
             right = onehot[g, :, i * 128 : (i + 2) * 128]
             found = dot(psi[...], jnp.concatenate([right, right], 0))
-            row = jnp.concatenate(
-                [recv[g * STEP + i + e, ROWS : ROWS + 1] for e in range(2)], 1
+            upper = jnp.concatenate(
+                [uppers[g * (STEP * 3 // 4) + i + e] for e in range(2)], 1
             )
-            upper = jnp.broadcast_to(jnp.floor(row * (1.0 / 256.0)), (ROWS, 256))
             value = jnp.zeros((ROWS, 256), F32)
             for j in range(KEPT // 2):
                 value = jnp.where(upper == float(j), found[j * ROWS : (j + 1) * ROWS], value)
-            for e in range(2):
-                sback[g * STEP + i + e] = value[:, e * 128 : (e + 1) * 128]
-
+            tiles += [value[:, :128], value[:, 128:]]
+        for i in range(0, STEP, 4):
+            three = tiles[i * 3 // 4 : i * 3 // 4 + 3]
+            for t in range(3):
+                sback[g * STEP + i + t] = three[t]
+            turned = [pltpu.roll(three[t], PART * (t + 1), 1) for t in range(3)]
+            sback[g * STEP + i + 3] = jnp.where(
+                lane < PART, turned[0], jnp.where(lane < 2 * PART, turned[1], turned[2])
+            )
         for i in range(STEP):
             if i > 0:
                 incoming(g, i).start()
@@ -433,7 +481,8 @@
     pair = jnp.concatenate(
         [arrived * phases[: PLANES * ROWS], arrived * phases[PLANES * ROWS :]], 0
     )
-    picked = dot3((lines_t[0], lines_t[1]), split(pair))
+    picked = pack(dot3((lines_t[0], lines_t[1]), split(pair)), pack_from) + terms[...]
+    picked = jnp.where(jnp.concatenate([live, live], 0), picked, 0.0)
     for part in range(2):
         rows = picked[part * DEPTH : (part + 1) * DEPTH].T
         back[part] = rows.reshape(GROUPS, SLOT, DEPTH)
@@ -443,7 +492,7 @@
         other = (tg + step) & (GROUPS - 1)
         copy = pltpu.make_async_remote_copy(
             src_ref=back.at[:, other],
-            dst_ref=picks.at[:, tg],
+            dst_ref=result.at[:, tg],
             send_sem=out_send.at[step],
             recv_sem=out_recv.at[step],
             device_id=(other, me),
@@ -451,26 +500,13 @@
         )
         copy.start()
         copies.append(copy)
-    column = own.T[:SLOT]
-    position = lax.broadcasted_iota(jnp.int32, (SLOT, DEPTH), 1).astype(F32)
-    live = position < column[:, 1:2]
-    height = position + column[:, 2:3]
-    height = jnp.where(height >= float(NG), height - float(NG), height)
-    height = jnp.where(height >= float(NG // 2), height - float(NG), height)
-    kinetic = (0.5 * (32.0 / (NG * NG))) * (column[:, 3:4] + height * height)
-    def add(band, value):
-        for part in range(2):
-            term = kinetic * coef[part, band]
-            result[part, band] = jnp.where(live, value[part] + term, 0.0)
-
-    add(tg, [back[0, tg], back[1, tg]])
-
+    own = pltpu.make_async_copy(back.at[:, tg], result.at[:, tg], stick_sem.at[0])
+    own.start()
     settle(send.at[pl.ds(1, PLANES - 1)], pl_send.at[0])
     settle(sback.at[pl.ds(1, PLANES - 1)], rt_send.at[0])
-    for step, copy in zip((1, 3, 2), copies[1:] + copies[:1]):
+    own.wait()
+    for copy in copies:
         copy.wait()
-        band = (tg - step) & (GROUPS - 1)
-        add(band, [picks[0, band], picks[1, band]])
 
 
 def local(coeffs, potential, stick_x, stick_y, stick_count, stick_offset):
@@ -482,7 +518,7 @@
         kernel,
         out_shape=jax.ShapeDtypeStruct((2, GROUPS, SLOT, DEPTH), F32),
         in_specs=[pl.BlockSpec(memory_space=pltpu.HBM)] * len(args),
-        out_specs=pl.BlockSpec(memory_space=pltpu.VMEM),
+        out_specs=pl.BlockSpec(memory_space=pltpu.HBM),
         scratch_shapes=[
             vmem(2, GROUPS, SLOT, DEPTH),
             vmem(2, GROUPS, SLOT, DEPTH),
@@ -496,7 +532,7 @@
             vmem(PLANES, ROWS + 1, 128),
             vmem(PLANES, ROWS + 1, 128),
             vmem(2 * PLANES * ROWS, 128),
-            vmem(PLANES // STEP, 2 * KEPT, STEP * 128, dtype=BF),
+            vmem(PLANES // STEP, 2 * KEPT, STEP * 96, dtype=BF),
             vmem(2, KEPT // 2 * ROWS, KEPT),
             vmem(2, KEPT // 2 * ROWS, KEPT),
             vmem(KEPT // 2 * ROWS, 4 * KEPT, dtype=BF),
@@ -504,7 +540,8 @@
             vmem(PLANES, ROWS, 128),
             vmem(PLANES, ROWS, 128),
             vmem(2, GROUPS, SLOT, DEPTH),
-            vmem(2, GROUPS, SLOT, DEPTH),
+            vmem(PLANES * 3 // 4, ROWS, 128),
+            vmem(2 * DEPTH, 128),
             dma((4,)),
             dma((10,)),
         ]

time: 49.4 us -> 48.5 us (0.982)
  Pallas kernels: 47.7 us -> 46.9 us
    pallas_call x1, Pallas kernels: 47.7 us -> 46.9 us  [local(): pl.pallas_call(kernel, out_shape=jax.ShapeDtypeStruct((2, GROUPS, SLOT, D...]
where the time goes in v2:
time: 48.5 us; the launch traced here: 48.4 us
  Pallas kernels  46.9 us (97%)
  local copies, waits for them, and re-layouts  1.57 us (3%)
    pallas_call x1, Pallas kernels, local(): pl.pallas_call(kernel, out_shape=jax.ShapeDtypeStruct((2, GROUPS, SLOT, D...  46.9 us
    unnamed x1, local copies, waits for them, and re-layouts  1.57 us

profile of v2, /device:TPU:1, one launch (start us, length us, event | category | flops | bytes accessed | tf_op | source)
XLA Modules:
  0.0 48.4 jit_solution(15659053556015436115)
XLA Ops:
  0.0 46.9 %shard_map.127 = f32[2,4,32,128]{3,2,1,0:T(8,128)} custom-call(f32[2,4,32,128]{3,2,1,0:T(8,128)} %coeffs.1, f32[4,256,256]{2,1,0:T(8,128)} %potential.1, s32[32]{0:T(128)} %stick_x.1, s32[32]{0:T(128)} %stick_y.1, s32[32]{0:T(128)} %stick_count.1, s32[32]{0:T(128)} %stick_offset.1, bf16[2,1024,256]{2,1,0:T(8,128)(2,1)} %constant.14.clone.lines_hbm, ...), custom_call_target="tpu_custom_call" | custom-call | tf_op jit(solution)/shard_map/pallas_call | solution.py:517
  46.9 1.6 %copy.15 = f32[2,4,32,128]{3,2,1,0:T(8,128)} copy(f32[2,4,32,128]{3,2,1,0:T(8,128)} %shard_map.127) | data formatting | bytes 262144

commit v3 on v2

--- a/solution.py
+++ b/solution.py
@@ -22,8 +22,7 @@
 ROWS = 2 * LAYERS
 KEPT = 128
 MAIN = 20
-LANES = GROUPS * MAIN + SLOT - MAIN
-PART = 32
+WIRE = 6
 STEP = 8
 
 
@@ -41,16 +40,12 @@
 
 @functools.lru_cache(None)
 def tables():
-    angle = angles(np.arange(NG), np.arange(DEPTH)).reshape(PLANES, LAYERS, DEPTH)
+    planes = np.add.outer(np.arange(LAYERS), LAYERS * np.arange(PLANES)).reshape(-1)
+    angle = angles(planes, np.arange(DEPTH))
     cos, sin = np.cos(angle), np.sin(angle)
-    real = np.concatenate([cos, -sin], -1)
-    imag = np.concatenate([sin, cos], -1)
-    straight = np.concatenate([real, imag], 1).reshape(-1, 2 * DEPTH)
-    turned = np.concatenate([-imag, real], 1).reshape(-1, 2 * DEPTH)
-    lines = np.concatenate([straight, turned])
-    angle = angles(np.arange(NG), np.arange(NG)).reshape(PLANES, LAYERS, NG)
-    double = lambda t: np.concatenate([t, t], 1).reshape(-1, NG)
-    phase = np.concatenate([double(np.cos(angle)), double(np.sin(angle))])
+    lines = np.block([[cos, -sin], [sin, cos]])
+    angle = angles(planes, np.arange(NG))
+    phase = np.concatenate([np.cos(angle), np.sin(angle)])
     freq = np.arange(KEPT) - KEPT // 2
     split = np.concatenate([freq[0::2], freq[1::2]])
     angle = angles(np.arange(NG), split)
@@ -132,7 +127,10 @@
     ayt,
     send,
     recv,
-    phases,
+    phase_a,
+    phase_b,
+    names,
+    idents,
     onehot,
     spread,
     plane,
@@ -145,6 +143,8 @@
     terms,
     stick_sem,
     local_sem,
+    id_send,
+    id_recv,
     tg_send,
     tg_recv,
     out_send,
@@ -216,16 +216,36 @@
 
     fetches[9].wait()
 
-    def packing(slot, lane):
+    def packing(slot, place):
         spot = slot & (SLOT - 1)
-        place = jnp.where(
-            spot < MAIN, (slot // SLOT) * MAIN + spot, spot + (GROUPS - 1) * MAIN
-        )
-        return jnp.where(place == lane, 1.0, 0.0).astype(BF)
+        own = jnp.where(spot < MAIN, (slot // SLOT) * MAIN + spot, spot + (GROUPS - 1) * MAIN)
+        return jnp.where(own == place, 1.0, 0.0).astype(BF)
 
     along = lax.broadcasted_iota(jnp.int32, (128, 128), 0)
     across = lax.broadcasted_iota(jnp.int32, (128, 128), 1)
-    pack_to, pack_from = packing(along, across), packing(across, along)
+    pack_to = jnp.concatenate(
+        [packing(along, across & 63), packing(along, 64 + (across & 31))], 1
+    )
+    pack_from = packing(across, along)
+    lane = lax.broadcasted_iota(jnp.int32, (ROWS, 128), 1)
+    sub = lax.broadcasted_iota(jnp.int32, (ROWS, 128), 0)
+    half = lane < 64
+    half1, quad1 = half[0:1], lane[0:1] // 32
+    quad = lane // 32
+    sign = jnp.where(half1, 1.0, -1.0)
+    swap = lambda v: pltpu.roll(v, 64, 1)
+
+    layer = sub & (LAYERS - 1)
+
+    def by_layer(values):
+        low = jnp.where(layer == 0, values[0], values[1])
+        return jnp.where(layer < 2, low, jnp.where(layer == 2, values[2], values[3]))
+
+    def diagonal(rows):
+        out = rows[0:PLANES]
+        for b in range(1, LAYERS):
+            out = jnp.where(quad1 == b, rows[b * PLANES : (b + 1) * PLANES], out)
+        return out
 
     copies = []
     for step in (2, 1, 3):
@@ -252,10 +272,37 @@
     count = info[1:2]
     packed = pack(info, pack_to)
     ids, offset = packed[0:1] - 1.0, packed[2:3]
+    names[0] = jnp.where(half1, ids[:, 0:128], ids[:, 128:256])
+
+    def peer(ring, spot, sign):
+        along_z = ((ring + 1) >> 1) * (2 * (ring & 1) - 1)
+        x = ((me >> 4) + sign * (spot >> 1)) & 3
+        z = ((me >> 1) + sign * along_z) & 7
+        return x * 16 + z * 2 + ((me + spot) & 1)
+
+    def introduce(ring, spot):
+        return pltpu.make_async_remote_copy(
+            src_ref=names.at[0],
+            dst_ref=idents.at[ring * STEP + spot],
+            send_sem=id_send.at[0],
+            recv_sem=id_recv.at[0],
+            device_id=(tg, peer(ring, spot, 1)),
+            device_id_type=MESH,
+        )
+
+    for ring in range(PLANES // STEP):
+        for spot in range(0 if ring else 1, STEP):
+            introduce(ring, spot).start()
+    idents[0] = names[0]
     fetches[1].wait()
     steps = lax.broadcasted_iota(jnp.int32, (NG, 128), 0).astype(F32)
-    chosen = jnp.where(steps == offset, 1.0, 0.0).astype(BF)
-    phases[...] = dot(phase[0], chosen) + dot(phase[1], chosen)
+    chosen = jnp.concatenate(
+        [jnp.where(steps == offset[:, t * 128 : (t + 1) * 128], 1.0, 0.0) for t in range(2)], 1
+    ).astype(BF)
+    turns = dot(phase[0], chosen) + dot(phase[1], chosen)
+    phase_a[...] = turns[:, :128]
+    for trig in range(2):
+        phase_b[trig] = diagonal(turns[trig * NG : (trig + 1) * NG, 128:])
     fetches[0].wait()
     fetches[2].wait()
     for copy in copies[1::2]:
@@ -267,25 +314,28 @@
         rows = group[part].reshape(GROUPS * SLOT, DEPTH)
         parts.append(jnp.where(live, rows.T, 0.0))
     masked = jnp.concatenate(parts, 0)
-    high, low = split(masked)
-    high, low = dot(high, pack_to).astype(BF), dot(low, pack_to).astype(BF)
-    both = dot3((lines[0], lines[1]), (high, low))
-    moved = both[: PLANES * ROWS] * phases[: PLANES * ROWS]
-    moved = moved + both[PLANES * ROWS :] * phases[PLANES * ROWS :]
-    send[:, 0:ROWS, :] = moved.reshape(PLANES, ROWS, 128)
-    send[:, ROWS : ROWS + 1, :] = jnp.broadcast_to(ids[None], (PLANES, 1, 128))
-
-    def peer(ring, spot, sign):
-        along_z = ((ring + 1) >> 1) * (2 * (ring & 1) - 1)
-        x = ((me >> 4) + sign * (spot >> 1)) & 3
-        z = ((me >> 1) + sign * along_z) & 7
-        return x * 16 + z * 2 + ((me + spot) & 1)
+    sides = []
+    for value in split(masked):
+        value = dot(value, pack_to)
+        re, im = value[:DEPTH, :128], value[DEPTH:, :128]
+        left = jnp.concatenate([jnp.where(half1, re, im), jnp.where(half1, im, -re)], 0)
+        sides.append(jnp.concatenate([left, value[:, 128:]], 1).astype(BF))
+    both = dot3((lines[0], lines[1]), sides)
+    moved = both[:NG, :128] * phase_a[:NG] - both[NG:, :128] * phase_a[NG:]
+    for z in range(LAYERS):
+        send[pl.ds(z, PLANES, stride=ROWS), :] = moved[z * PLANES : (z + 1) * PLANES]
+    re, im = diagonal(both[:NG, 128:]), diagonal(both[NG:, 128:])
+    send[pl.ds(LAYERS, PLANES, stride=ROWS), :] = re * phase_b[0] - im * phase_b[1]
+    send[pl.ds(LAYERS + 1, PLANES, stride=ROWS), :] = im * phase_b[0] + re * phase_b[1]
+
+    def spot_rows(index, rows):
+        return pl.ds(pl.multiple_of(index * ROWS, ROWS), rows)
 
     def outgoing(ring, spot):
         other = peer(ring, spot, 1)
         return pltpu.make_async_remote_copy(
-            src_ref=send.at[other],
-            dst_ref=recv.at[ring * STEP + spot],
+            src_ref=send.at[spot_rows(other, WIRE)],
+            dst_ref=recv.at[spot_rows(ring * STEP + spot, WIRE)],
             send_sem=pl_send.at[0],
             recv_sem=pl_recv.at[ring],
             device_id=(tg, other),
@@ -295,7 +345,7 @@
     for ring in range(PLANES // STEP):
         for spot in range(0 if ring else 1, STEP):
             outgoing(ring, spot).start()
-    recv[0] = send[me]
+    recv[0:ROWS] = send[spot_rows(me, ROWS)]
 
     height = steps[:DEPTH] + info[2:3]
     height = jnp.where(height >= float(NG), height - float(NG), height)
@@ -307,30 +357,48 @@
     second = jnp.where(lax.broadcasted_iota(jnp.int32, (16, 128), 0) >= 8, 1.0, 0.0).astype(F32)
     one, zero = jnp.ones((), BF), jnp.zeros((), BF)
 
-    lane9 = lax.broadcasted_iota(jnp.int32, (ROWS + 1, 128), 1)
+    settle(idents.at[pl.ds(1, PLANES - 1)], id_recv.at[0])
 
     def place(g, carry):
         @pl.when(g == 0)
         def _():
-            settle(recv.at[pl.ds(1, STEP - 1)], pl_recv.at[0])
+            settle(recv.at[pl.ds(0, (STEP - 1) * WIRE)], pl_recv.at[0])
 
         @pl.when(g > 0)
         def _():
-            settle(recv.at[pl.ds(g * STEP, STEP)], pl_recv.at[g])
-
-        block = recv[pl.ds(g * STEP, STEP)]
+            settle(recv.at[pl.ds(0, STEP * WIRE)], pl_recv.at[g])
+
+        block = recv[spot_rows(g * STEP, STEP * ROWS)]
+        names8 = idents[pl.ds(g * STEP, STEP)]
         left, right = [], []
         tiles = []
         for i in range(0, STEP, 4):
-            for t in range(3):
-                spread_out = pltpu.roll(block[i + 3], 96 - PART * t, 1)
-                tiles.append(jnp.where(lane9 < 96, block[i + t], spread_out))
-        for i, tile in enumerate(tiles):
-            high, low = split(tile[0:ROWS])
-            row = tile[ROWS : ROWS + 1]
-            upper = jnp.floor(row * (1.0 / 256.0))
-            lower = (row - 256.0 * upper).astype(BF)
-            uppers[g * len(tiles) + i] = jnp.broadcast_to(upper, (ROWS, 128))
+            rows = [block[(i + j) * ROWS : (i + j + 1) * ROWS] for j in range(4)]
+            ids8 = [jnp.broadcast_to(names8[i + j], (ROWS, 128)) for j in range(4)]
+            for a in (0, 2):
+                top = jnp.where(half, rows[a], swap(rows[a + 1]))
+                low = jnp.where(half, swap(rows[a]), rows[a + 1])
+                tile = jnp.where(sub < LAYERS, top, pltpu.roll(low, LAYERS, 0))
+                tiles.append((tile, jnp.where(half, ids8[a], swap(ids8[a + 1]))))
+            wide = [
+                jnp.where(sub < LAYERS, row[LAYERS : LAYERS + 1], row[LAYERS + 1 : LAYERS + 2])
+                for row in rows
+            ]
+            name = jnp.zeros((ROWS, 128), F32)
+            for j in range(4):
+                near = ids8[j] if j == 2 else pltpu.roll(ids8[j], (32 * j - 64) % 128, 1)
+                name = jnp.where(quad == j, near, name)
+            tile = by_layer(wide)
+            for d in range(1, 4):
+                shifted = pltpu.roll(by_layer(wide[d:] + wide[:d]), 32 * d, 1)
+                tile = jnp.where(quad == (layer + d) & 3, shifted, tile)
+            tiles.append((tile, name))
+        for i, (tile, name) in enumerate(tiles):
+            high, low = split(tile)
+            upper = jnp.floor(name * (1.0 / 256.0))
+            lower = (name - 256.0 * upper)[0:1].astype(BF)
+            uppers[g * len(tiles) + i] = upper
+            upper = jnp.concatenate([upper, upper], 0)
             match = (upper - second).astype(BF)
             pieces = []
             for value in (high, low):
@@ -345,8 +413,7 @@
         total = lax.dot_general(
             left, right, (((1,), (1,)), ((), ())), preferred_element_type=F32
         )
-        half = KEPT // 2 * ROWS
-        total = total[:half] + total[half:]
+        total = total[: KEPT // 2 * ROWS] + total[KEPT // 2 * ROWS :]
 
         @pl.when(g == 0)
         def _():
@@ -363,7 +430,6 @@
     lax.fori_loop(0, PLANES // STEP, place, 0)
 
     corner = spread[0, 0:ROWS]
-    lane = lax.broadcasted_iota(jnp.int32, (ROWS, 128), 1)
     edge_x = jnp.where(lane == 0, corner, 0.0).sum(axis=1, keepdims=True)
     edge_y = jnp.where(lane == 1, corner, 0.0).sum(axis=1, keepdims=True)
     spread[0, 0:ROWS] = jnp.where(lane < 2, 0.0, corner)
@@ -432,8 +498,8 @@
     def incoming(ring, spot):
         other = peer(ring, spot, -1)
         return pltpu.make_async_remote_copy(
-            src_ref=sback.at[ring * STEP + spot],
-            dst_ref=ret.at[me],
+            src_ref=sback.at[spot_rows(ring * STEP + spot, WIRE)],
+            dst_ref=ret.at[spot_rows(me, WIRE)],
             send_sem=rt_send.at[0],
             recv_sem=rt_recv.at[0],
             device_id=(tg, other),
@@ -454,13 +520,21 @@
                 value = jnp.where(upper == float(j), found[j * ROWS : (j + 1) * ROWS], value)
             tiles += [value[:, :128], value[:, 128:]]
         for i in range(0, STEP, 4):
-            three = tiles[i * 3 // 4 : i * 3 // 4 + 3]
-            for t in range(3):
-                sback[g * STEP + i + t] = three[t]
-            turned = [pltpu.roll(three[t], PART * (t + 1), 1) for t in range(3)]
-            sback[g * STEP + i + 3] = jnp.where(
-                lane < PART, turned[0], jnp.where(lane < 2 * PART, turned[1], turned[2])
-            )
+            pairs = []
+            for a in range(2):
+                tile = tiles[i * 3 // 4 + a]
+                lower = pltpu.roll(tile, LAYERS, 0)
+                pairs.append(jnp.where(half, tile, swap(lower)))
+                pairs.append(jnp.where(half, swap(tile), lower))
+            tile = tiles[i * 3 // 4 + 2]
+            shifts = [tile] + [pltpu.roll(tile, 128 - 32 * d, 1) for d in range(1, 4)]
+            for j in range(4):
+                turned = by_layer([shifts[(j - b) & 3] for b in range(LAYERS)])
+                turned = jnp.where(quad == layer, turned, 0.0)
+                re = turned[:LAYERS].sum(axis=0, keepdims=True)
+                im = turned[LAYERS:].sum(axis=0, keepdims=True)
+                out = jnp.where(sub < LAYERS, pairs[j], jnp.where(sub == LAYERS, re, im))
+                sback[spot_rows(g * STEP + i + j, ROWS)] = out
         for i in range(STEP):
             if i > 0:
                 incoming(g, i).start()
@@ -473,15 +547,33 @@
         return carry
 
     lax.fori_loop(0, PLANES // STEP, pick, 0)
-    ret[me] = sback[0]
-
-    settle(ret.at[pl.ds(1, PLANES - 1)], rt_recv.at[0])
+    ret[spot_rows(me, ROWS)] = sback[0:ROWS]
+
+    settle(ret.at[pl.ds(0, (PLANES - 1) * WIRE)], rt_recv.at[0])
     fetches[8].wait()
-    arrived = ret[...].reshape(PLANES * ROWS, 128)
-    pair = jnp.concatenate(
-        [arrived * phases[: PLANES * ROWS], arrived * phases[PLANES * ROWS :]], 0
+    lead = jnp.concatenate([ret[pl.ds(z, PLANES, stride=ROWS), :] for z in range(LAYERS)], 0)
+    lead = lead * phase_a[:NG] + swap(lead) * (phase_a[NG:] * sign)
+    rest_re = ret[pl.ds(LAYERS, PLANES, stride=ROWS), :]
+    rest_im = ret[pl.ds(LAYERS + 1, PLANES, stride=ROWS), :]
+    rest = []
+    for value in (
+        rest_re * phase_b[0] + rest_im * phase_b[1],
+        rest_im * phase_b[0] - rest_re * phase_b[1],
+    ):
+        rest += [jnp.where(quad1 == b, value, 0.0) for b in range(LAYERS)]
+    lead = dot3((lines_t[0, :, :NG], lines_t[1, :, :NG]), split(lead))
+    lead = lead[:DEPTH] - swap(lead[DEPTH:]) * sign
+    rest = dot3((lines_t[0], lines_t[1]), split(jnp.concatenate(rest, 0)))
+    rest = rest + swap(rest)
+    rest = rest + pltpu.roll(rest, 32, 1)
+    picked = jnp.concatenate(
+        [
+            jnp.where(half1, lead, rest[:DEPTH]),
+            jnp.where(half1, swap(lead), rest[DEPTH:]),
+        ],
+        0,
     )
-    picked = pack(dot3((lines_t[0], lines_t[1]), split(pair)), pack_from) + terms[...]
+    picked = pack(picked, pack_from) + terms[...]
     picked = jnp.where(jnp.concatenate([live, live], 0), picked, 0.0)
     for part in range(2):
         rows = picked[part * DEPTH : (part + 1) * DEPTH].T
@@ -502,8 +594,9 @@
         copies.append(copy)
     own = pltpu.make_async_copy(back.at[:, tg], result.at[:, tg], stick_sem.at[0])
     own.start()
-    settle(send.at[pl.ds(1, PLANES - 1)], pl_send.at[0])
-    settle(sback.at[pl.ds(1, PLANES - 1)], rt_send.at[0])
+    settle(idents.at[pl.ds(1, PLANES - 1)], id_send.at[0])
+    settle(send.at[pl.ds(0, (PLANES - 1) * WIRE)], pl_send.at[0])
+    settle(sback.at[pl.ds(0, (PLANES - 1) * WIRE)], rt_send.at[0])
     own.wait()
     for copy in copies:
         copy.wait()
@@ -529,21 +622,26 @@
         ]
         + [vmem(*t.shape, dtype=BF) for t in consts]
         + [
-            vmem(PLANES, ROWS + 1, 128),
-            vmem(PLANES, ROWS + 1, 128),
-            vmem(2 * PLANES * ROWS, 128),
+            vmem(PLANES * ROWS, 128),
+            vmem(PLANES * ROWS, 128),
+            vmem(2 * NG, 128),
+            vmem(2, PLANES, 128),
+            vmem(1, 1, 128),
+            vmem(PLANES, 1, 128),
             vmem(PLANES // STEP, 2 * KEPT, STEP * 96, dtype=BF),
             vmem(2, KEPT // 2 * ROWS, KEPT),
             vmem(2, KEPT // 2 * ROWS, KEPT),
             vmem(KEPT // 2 * ROWS, 4 * KEPT, dtype=BF),
             vmem(2 * NG, LAYERS * KEPT),
-            vmem(PLANES, ROWS, 128),
-            vmem(PLANES, ROWS, 128),
+            vmem(PLANES * ROWS, 128),
+            vmem(PLANES * ROWS, 128),
             vmem(2, GROUPS, SLOT, DEPTH),
             vmem(PLANES * 3 // 4, ROWS, 128),
             vmem(2 * DEPTH, 128),
             dma((4,)),
             dma((10,)),
+            dma((1,)),
+            dma((1,)),
         ]
         + [dma((GROUPS,))] * 6
         + [dma((1,)), dma((PLANES // STEP,)), dma((1,)), dma((1,))],

time: 48.5 us -> 47 us (0.969)
  Pallas kernels: 46.9 us -> 45.4 us
    pallas_call x1, Pallas kernels: 46.9 us -> 45.4 us  [local(): pl.pallas_call(kernel, out_shape=jax.ShapeDtypeStruct((2, GROUPS, SLOT, D...]
where the time goes in v3:
time: 47 us; the launch traced here: 46.9 us
  Pallas kernels  45.4 us (97%)
  local copies, waits for them, and re-layouts  1.57 us (3%)
    pallas_call x1, Pallas kernels, local(): pl.pallas_call(kernel, out_shape=jax.ShapeDtypeStruct((2, GROUPS, SLOT, D...  45.4 us
    unnamed x1, local copies, waits for them, and re-layouts  1.57 us

profile of v3, /device:TPU:1, one launch (start us, length us, event | category | flops | bytes accessed | tf_op | source)
XLA Modules:
  0.0 46.9 jit_solution(17188712627117190195)
XLA Ops:
  0.0 45.4 %shard_map.127 = f32[2,4,32,128]{3,2,1,0:T(8,128)} custom-call(f32[2,4,32,128]{3,2,1,0:T(8,128)} %coeffs.1, f32[4,256,256]{2,1,0:T(8,128)} %potential.1, s32[32]{0:T(128)} %stick_x.1, s32[32]{0:T(128)} %stick_y.1, s32[32]{0:T(128)} %stick_count.1, s32[32]{0:T(128)} %stick_offset.1, bf16[2,512,256]{2,1,0:T(8,128)(2,1)} %constant.14.clone.lines_hbm, ...), custom_call_target="tpu_custom_call" | custom-call | tf_op jit(solution)/shard_map/pallas_call | solution.py:610
  45.4 1.6 %copy.15 = f32[2,4,32,128]{3,2,1,0:T(8,128)} copy(f32[2,4,32,128]{3,2,1,0:T(8,128)} %shard_map.127) | data formatting | bytes 262144

commit v4 on v3

--- a/solution.py
+++ b/solution.py
@@ -129,8 +129,6 @@
     recv,
     phase_a,
     phase_b,
-    names,
-    idents,
     onehot,
     spread,
     plane,
@@ -143,8 +141,6 @@
     terms,
     stick_sem,
     local_sem,
-    id_send,
-    id_recv,
     tg_send,
     tg_recv,
     out_send,
@@ -179,7 +175,7 @@
         pltpu.make_async_copy(src, sticks.at[i], stick_sem.at[i])
         for i, src in enumerate((stick_x, stick_y, stick_count, stick_offset))
     ]
-    for fetch in rows + fetches[9:] + fetches[:9]:
+    for fetch in rows + fetches[9:]:
         fetch.start()
 
     barrier = pltpu.get_barrier_semaphore()
@@ -195,6 +191,8 @@
         return carry
 
     lax.fori_loop(1, PLANES, greet, 0, unroll=True)
+    for fetch in fetches[:9]:
+        fetch.start()
     for row in rows:
         row.wait()
     mine = sticks[...]
@@ -272,7 +270,7 @@
     count = info[1:2]
     packed = pack(info, pack_to)
     ids, offset = packed[0:1] - 1.0, packed[2:3]
-    names[0] = jnp.where(half1, ids[:, 0:128], ids[:, 128:256])
+    names = jnp.where(half1, ids[:, 0:128], ids[:, 128:256])
 
     def peer(ring, spot, sign):
         along_z = ((ring + 1) >> 1) * (2 * (ring & 1) - 1)
@@ -280,20 +278,6 @@
         z = ((me >> 1) + sign * along_z) & 7
         return x * 16 + z * 2 + ((me + spot) & 1)
 
-    def introduce(ring, spot):
-        return pltpu.make_async_remote_copy(
-            src_ref=names.at[0],
-            dst_ref=idents.at[ring * STEP + spot],
-            send_sem=id_send.at[0],
-            recv_sem=id_recv.at[0],
-            device_id=(tg, peer(ring, spot, 1)),
-            device_id_type=MESH,
-        )
-
-    for ring in range(PLANES // STEP):
-        for spot in range(0 if ring else 1, STEP):
-            introduce(ring, spot).start()
-    idents[0] = names[0]
     fetches[1].wait()
     steps = lax.broadcasted_iota(jnp.int32, (NG, 128), 0).astype(F32)
     chosen = jnp.concatenate(
@@ -327,6 +311,7 @@
     re, im = diagonal(both[:NG, 128:]), diagonal(both[NG:, 128:])
     send[pl.ds(LAYERS, PLANES, stride=ROWS), :] = re * phase_b[0] - im * phase_b[1]
     send[pl.ds(LAYERS + 1, PLANES, stride=ROWS), :] = im * phase_b[0] + re * phase_b[1]
+    send[pl.ds(WIRE, PLANES, stride=ROWS), :] = jnp.broadcast_to(names, (PLANES, 128))
 
     def spot_rows(index, rows):
         return pl.ds(pl.multiple_of(index * ROWS, ROWS), rows)
@@ -334,8 +319,8 @@
     def outgoing(ring, spot):
         other = peer(ring, spot, 1)
         return pltpu.make_async_remote_copy(
-            src_ref=send.at[spot_rows(other, WIRE)],
-            dst_ref=recv.at[spot_rows(ring * STEP + spot, WIRE)],
+            src_ref=send.at[spot_rows(other, WIRE + 1)],
+            dst_ref=recv.at[spot_rows(ring * STEP + spot, WIRE + 1)],
             send_sem=pl_send.at[0],
             recv_sem=pl_recv.at[ring],
             device_id=(tg, other),
@@ -347,34 +332,25 @@
             outgoing(ring, spot).start()
     recv[0:ROWS] = send[spot_rows(me, ROWS)]
 
-    height = steps[:DEPTH] + info[2:3]
-    height = jnp.where(height >= float(NG), height - float(NG), height)
-    height = jnp.where(height >= float(NG // 2), height - float(NG), height)
-    kinetic = (0.5 * (32.0 / (NG * NG))) * (info[3:4] + height * height)
-    terms[...] = jnp.concatenate([kinetic, kinetic], 0) * masked
-
     column = lax.broadcasted_iota(jnp.int32, (2 * KEPT, 128), 0).astype(F32).astype(BF)
     second = jnp.where(lax.broadcasted_iota(jnp.int32, (16, 128), 0) >= 8, 1.0, 0.0).astype(F32)
     one, zero = jnp.ones((), BF), jnp.zeros((), BF)
 
-    settle(idents.at[pl.ds(1, PLANES - 1)], id_recv.at[0])
-
     def place(g, carry):
         @pl.when(g == 0)
         def _():
-            settle(recv.at[pl.ds(0, (STEP - 1) * WIRE)], pl_recv.at[0])
+            settle(recv.at[pl.ds(0, (STEP - 1) * (WIRE + 1))], pl_recv.at[0])
 
         @pl.when(g > 0)
         def _():
-            settle(recv.at[pl.ds(0, STEP * WIRE)], pl_recv.at[g])
+            settle(recv.at[pl.ds(0, STEP * (WIRE + 1))], pl_recv.at[g])
 
         block = recv[spot_rows(g * STEP, STEP * ROWS)]
-        names8 = idents[pl.ds(g * STEP, STEP)]
         left, right = [], []
         tiles = []
         for i in range(0, STEP, 4):
             rows = [block[(i + j) * ROWS : (i + j + 1) * ROWS] for j in range(4)]
-            ids8 = [jnp.broadcast_to(names8[i + j], (ROWS, 128)) for j in range(4)]
+            ids8 = [jnp.broadcast_to(rows[j][WIRE : WIRE + 1], (ROWS, 128)) for j in range(4)]
             for a in (0, 2):
                 top = jnp.where(half, rows[a], swap(rows[a + 1]))
                 low = jnp.where(half, swap(rows[a]), rows[a + 1])
@@ -549,6 +525,12 @@
     lax.fori_loop(0, PLANES // STEP, pick, 0)
     ret[spot_rows(me, ROWS)] = sback[0:ROWS]
 
+    height = steps[:DEPTH] + info[2:3]
+    height = jnp.where(height >= float(NG), height - float(NG), height)
+    height = jnp.where(height >= float(NG // 2), height - float(NG), height)
+    kinetic = (0.5 * (32.0 / (NG * NG))) * (info[3:4] + height * height)
+    terms[...] = jnp.concatenate([kinetic, kinetic], 0) * masked
+
     settle(ret.at[pl.ds(0, (PLANES - 1) * WIRE)], rt_recv.at[0])
     fetches[8].wait()
     lead = jnp.concatenate([ret[pl.ds(z, PLANES, stride=ROWS), :] for z in range(LAYERS)], 0)
@@ -594,8 +576,7 @@
         copies.append(copy)
     own = pltpu.make_async_copy(back.at[:, tg], result.at[:, tg], stick_sem.at[0])
     own.start()
-    settle(idents.at[pl.ds(1, PLANES - 1)], id_send.at[0])
-    settle(send.at[pl.ds(0, (PLANES - 1) * WIRE)], pl_send.at[0])
+    settle(send.at[pl.ds(0, (PLANES - 1) * (WIRE + 1))], pl_send.at[0])
     settle(sback.at[pl.ds(0, (PLANES - 1) * WIRE)], rt_send.at[0])
     own.wait()
     for copy in copies:
@@ -626,8 +607,6 @@
             vmem(PLANES * ROWS, 128),
             vmem(2 * NG, 128),
             vmem(2, PLANES, 128),
-            vmem(1, 1, 128),
-            vmem(PLANES, 1, 128),
             vmem(PLANES // STEP, 2 * KEPT, STEP * 96, dtype=BF),
             vmem(2, KEPT // 2 * ROWS, KEPT),
             vmem(2, KEPT // 2 * ROWS, KEPT),
@@ -640,8 +619,6 @@
             vmem(2 * DEPTH, 128),
             dma((4,)),
             dma((10,)),
-            dma((1,)),
-            dma((1,)),
         ]
         + [dma((GROUPS,))] * 6
         + [dma((1,)), dma((PLANES // STEP,)), dma((1,)), dma((1,))],

time: 47 us -> 46.2 us (0.983)
  Pallas kernels: 45.4 us -> 44.5 us
    pallas_call x1, Pallas kernels: 45.4 us -> 44.5 us  [local(): pl.pallas_call(kernel, out_shape=jax.ShapeDtypeStruct((2, GROUPS, SLOT, D...]
where the time goes in v4:
time: 46.2 us; the launch traced here: 46.1 us
  Pallas kernels  44.5 us (96%)
  local copies, waits for them, and re-layouts  1.57 us (3%)
    pallas_call x1, Pallas kernels, local(): pl.pallas_call(kernel, out_shape=jax.ShapeDtypeStruct((2, GROUPS, SLOT, D...  44.5 us
    unnamed x1, local copies, waits for them, and re-layouts  1.57 us

profile of v4, /device:TPU:1, one launch (start us, length us, event | category | flops | bytes accessed | tf_op | source)
XLA Modules:
  0.0 46.1 jit_solution(2363012983797486348)
XLA Ops:
  0.0 44.5 %shard_map.127 = f32[2,4,32,128]{3,2,1,0:T(8,128)} custom-call(f32[2,4,32,128]{3,2,1,0:T(8,128)} %coeffs.1, f32[4,256,256]{2,1,0:T(8,128)} %potential.1, s32[32]{0:T(128)} %stick_x.1, s32[32]{0:T(128)} %stick_y.1, s32[32]{0:T(128)} %stick_count.1, s32[32]{0:T(128)} %stick_offset.1, bf16[2,512,256]{2,1,0:T(8,128)(2,1)} %constant.14.clone.lines_hbm, ...), custom_call_target="tpu_custom_call" | custom-call | tf_op jit(solution)/shard_map/pallas_call | solution.py:591
  44.5 1.6 %copy.15 = f32[2,4,32,128]{3,2,1,0:T(8,128)} copy(f32[2,4,32,128]{3,2,1,0:T(8,128)} %shard_map.127) | data formatting | bytes 262144

commit v5 on v4

--- a/solution.py
+++ b/solution.py
@@ -328,7 +328,7 @@
         )
 
     for ring in range(PLANES // STEP):
-        for spot in range(0 if ring else 1, STEP):
+        for spot in (4, 5, 6, 7, 2, 3, 1, 0)[: STEP if ring else STEP - 1]:
             outgoing(ring, spot).start()
     recv[0:ROWS] = send[spot_rows(me, ROWS)]
 
@@ -511,7 +511,7 @@
                 im = turned[LAYERS:].sum(axis=0, keepdims=True)
                 out = jnp.where(sub < LAYERS, pairs[j], jnp.where(sub == LAYERS, re, im))
                 sback[spot_rows(g * STEP + i + j, ROWS)] = out
-        for i in range(STEP):
+        for i in (4, 5, 6, 7, 2, 3, 1, 0):
             if i > 0:
                 incoming(g, i).start()
             else:

time: 46.2 us -> 45.7 us (0.989)
  Pallas kernels: 44.5 us -> 44 us
    pallas_call x1, Pallas kernels: 44.5 us -> 44 us  [local(): pl.pallas_call(kernel, out_shape=jax.ShapeDtypeStruct((2, GROUPS, SLOT, D...]
where the time goes in v5:
time: 45.7 us; the launch traced here: 45.6 us
  Pallas kernels  44 us (96%)
  local copies, waits for them, and re-layouts  1.57 us (3%)
    pallas_call x1, Pallas kernels, local(): pl.pallas_call(kernel, out_shape=jax.ShapeDtypeStruct((2, GROUPS, SLOT, D...  44 us
    unnamed x1, local copies, waits for them, and re-layouts  1.57 us

profile of v5, /device:TPU:1, one launch (start us, length us, event | category | flops | bytes accessed | tf_op | source)
XLA Modules:
  0.0 45.6 jit_solution(9481151887497088688)
XLA Ops:
  0.0 44.0 %shard_map.127 = f32[2,4,32,128]{3,2,1,0:T(8,128)} custom-call(f32[2,4,32,128]{3,2,1,0:T(8,128)} %coeffs.1, f32[4,256,256]{2,1,0:T(8,128)} %potential.1, s32[32]{0:T(128)} %stick_x.1, s32[32]{0:T(128)} %stick_y.1, s32[32]{0:T(128)} %stick_count.1, s32[32]{0:T(128)} %stick_offset.1, bf16[2,512,256]{2,1,0:T(8,128)(2,1)} %constant.14.clone.lines_hbm, ...), custom_call_target="tpu_custom_call" | custom-call | tf_op jit(solution)/shard_map/pallas_call | solution.py:591
  44.0 1.6 %copy.15 = f32[2,4,32,128]{3,2,1,0:T(8,128)} copy(f32[2,4,32,128]{3,2,1,0:T(8,128)} %shard_map.127) | data formatting | bytes 262144
